TPU v7x, 32 devices: a whole 2x2x4 slice. The times are simulated.
32 devices in a mesh: seq: 16 (over z, x, core), head: 2 (over y).
Axes of the slice: x: 2, y: 2, z: 4, core: 2. Of those that a mesh axis runs over, the one named last changes fastest.
Arguments:
- query_input: bfloat16 [14336, 4096], P(('seq', 'head')), may hold values from -12 to 12
- encoded_keys: bfloat16 [14336, 1024], P(('seq', 'head')), may hold values from -8 to 8
- input_values: bfloat16 [14336, 1024], P(('seq', 'head')), may hold values from -6 to 6
- sources: int32 [16, 3], P('seq'), may hold values from -1 to 14, as said below
Outputs:
- attended: bfloat16 [14336, 4096], P(('seq', 'head'))
Inputs may be any that keep to these rules, and one draw needn't show every extreme that they name: `sources`: row c: column 0 is c - 1; columns 1 and 2 are c - 2**a and c - 2**b for two different a, b >= 1 with 2**a and 2**b below 16; an entry is -1 where that value is negative.
All inputs are finite; a program needn't handle non-finite values.
Results may differ from a plain program's by a relative error of at most 0.006.
Values may be sent and summed in bfloat16 or wider, within the bound.
A program may use at most 64 MiB of HBM per device.

v0:
```python
from functools import reduce

import jax
import jax.numpy as jnp
from jax import lax
from jax.sharding import PartitionSpec as P

HEAD_SIZE = 128


negative_fill = -1e30


def passed_along(value, axis, by):
    devices = lax.axis_size(axis)
    pairs = [(i, i + by) for i in range(devices) if 0 <= i + by < devices]
    return lax.ppermute(value, axis, pairs)


def block_terms(query_head, key_head, value_head, causal):
    scores = lax.dot_general(
        query_head, key_head, (((1,), (1,)), ((), ())), preferred_element_type=jnp.float32
    ) * HEAD_SIZE ** (-0.5)
    if causal:
        position = jnp.arange(query_head.shape[0])
        allowed = position[:, None] >= position[None, :]
        scores = jnp.where(allowed, scores, negative_fill)
    highest = jnp.max(scores, axis=-1)
    weights = jnp.exp(scores - highest[:, None]).astype(jnp.bfloat16)
    row_total = jnp.sum(weights.astype(jnp.float32), axis=-1)
    partial_out = jnp.dot(weights, value_head, preferred_element_type=jnp.float32)
    return (highest, row_total, partial_out)


def combine(block_list, validity):
    maxima = [
        jnp.where(is_valid, block_term[0], negative_fill)
        for block_term, is_valid in zip(block_list, validity)
    ]
    overall = reduce(jnp.maximum, maxima)
    weighted = jnp.zeros(block_list[0][2].shape, jnp.float32)
    normalizer = jnp.zeros(block_list[0][1].shape, jnp.float32)
    for block_term, is_valid in zip(block_list, validity):
        factor = jnp.where(is_valid, jnp.exp(block_term[0] - overall), 0.0)
        weighted = weighted + factor[:, None] * block_term[2]
        normalizer = normalizer + factor * block_term[1]
    return weighted / normalizer[:, None]


def per_device(query_input, encoded_keys, input_values, sources):
    local_query, local_key, local_value = (
        lax.all_to_all(query_input, "head", split_axis=1, concat_axis=0, tiled=True),
        lax.all_to_all(encoded_keys, "head", split_axis=1, concat_axis=0, tiled=True),
        lax.all_to_all(input_values, "head", split_axis=1, concat_axis=0, tiled=True),
    )
    length = local_query.shape[0]
    query_heads = local_query.shape[1] // HEAD_SIZE
    key_value = jnp.stack([local_key, local_value])
    column_heads = key_value.shape[2] // HEAD_SIZE
    sharing = query_heads // column_heads
    span_count = lax.axis_size("seq")
    own_index = lax.axis_index("seq")
    previous = passed_along(key_value, "seq", 1)
    distances = [2**power for power in range(1, 31) if 2**power < span_count]
    fetched = [passed_along(key_value, "seq", distance) for distance in distances]
    source_row = sources[0]
    distance_table = jnp.array(distances, jnp.int32)

    def select_far(column):
        distance_away = own_index - source_row[column]
        slot_number = jnp.sum((distance_table < distance_away).astype(jnp.int32))
        chosen = fetched[0]
        for candidate_number in range(1, len(fetched)):
            chosen = jnp.where(slot_number == candidate_number, fetched[candidate_number], chosen)
        return chosen

    remotes = [
        (previous, source_row[0] >= 0),
        (select_far(1), source_row[1] >= 0),
        (select_far(2), source_row[2] >= 0),
    ]

    def one_head(head_number):
        query_head = lax.dynamic_slice_in_dim(local_query, head_number * HEAD_SIZE, HEAD_SIZE, 1)
        offset = head_number // sharing * HEAD_SIZE
        own_key = lax.dynamic_slice_in_dim(key_value[0], offset, HEAD_SIZE, 1)
        own_value = lax.dynamic_slice_in_dim(key_value[1], offset, HEAD_SIZE, 1)
        block_list = [block_terms(query_head, own_key, own_value, True)]
        validity = [jnp.array(True)]
        for remote, is_valid in remotes:
            key_head = lax.dynamic_slice_in_dim(remote[0], offset, HEAD_SIZE, 1)
            value_head = lax.dynamic_slice_in_dim(remote[1], offset, HEAD_SIZE, 1)
            block_term = block_terms(query_head, key_head, value_head, False)
            block_list.append(block_term)
            validity.append(is_valid)
        return combine(block_list, validity).astype(jnp.bfloat16)

    def write_head(head_number, output):
        return lax.dynamic_update_slice_in_dim(
            output, one_head(head_number), head_number * HEAD_SIZE, 1
        )

    attended = lax.fori_loop(
        0, query_heads, write_head, jnp.zeros((length, query_heads * HEAD_SIZE), jnp.bfloat16)
    )
    return lax.all_to_all(attended, "head", split_axis=0, concat_axis=1, tiled=True)


def solution(mesh):
    in_specs = (
        P(("seq", "head"), None),
        P(("seq", "head"), None),
        P(("seq", "head"), None),
        P("seq", None),
    )
    out_specs = P(("seq", "head"), None)
    return jax.shard_map(
        per_device, mesh=mesh, in_specs=in_specs, out_specs=out_specs, check_vma=False
    )
```

profile of v0, /device:TPU:16, one launch (start us, length us, event | category | flops | bytes accessed | tf_op | source)
XLA Modules:
  0.0 508.5 jit_solution(16080534457953014040)
XLA Ops:
  0.0 2.3 copy.26
  2.3 3.6 all-to-all-start.1
  5.9 12.4 %all-to-all-done.1 = bf16[448,2,512]{2,0,1:T(8,128)(2,1)S(1)} async-done(((bf16[448,2,512]{2,0,1:T(8,128)(2,1)}), bf16[448,2,512]{2,0,1:T(8,128)(2,1)S(1)}, u32[]{:S(2)}, u32[]{:S(2)}) %all-to-all-start.1) | async-done | bytes 917536 | tf_op jit(solution)/shard_map/all_to_all | solution.py:53
  18.3 14.3 %all_to_all.76 = bf16[448,2,512]{2,0,1:T(8,128)(2,1)S(1)} all-to-all(bf16[448,2,512]{2,0,1:T(8,128)(2,1)S(1)} %bitcast.76), channel_id=1, replica_groups=mesh['seq'=16,'head'=2] {'head'}, dimensions={1} | all-to-all | bytes 1835008 | tf_op jit(solution)/shard_map/all_to_all | solution.py:54
  36.2 3.5 collective-permute-start.2
  39.7 3.4 collective-permute-start.3
  43.1 2.3 copy.24
  45.4 5.5 %all-to-all-start = ((bf16[448,2,2048]{2,0,1:T(8,128)(2,1)}), bf16[448,2,2048]{2,0,1:T(8,128)(2,1)}, u32[]{:S(2)}, u32[]{:S(2)}) async-start(bf16[448,2,2048]{2,0,1:T(8,128)(2,1)} %bitcast.68), calls=%async_computation | async-start | bytes 7340032 | tf_op jit(solution)/shard_map/all_to_all | solution.py:52
  51.0 1.9 collective-permute-start
  59.5 21.4 %collective-permute-done.1 = bf16[2,896,512]{2,1,0:T(8,128)(2,1)S(1)} collective-permute-done((bf16[2,896,512]{2,1,0:T(8,128)(2,1)}, bf16[2,896,512]{2,1,0:T(8,128)(2,1)S(1)}, u32[]{:S(2)}, u32[]{:S(2)}) %collective-permute-start.1) | collective-permute-done | bytes 1835040 | tf_op jit(solution)/shard_map/ppermute | solution.py:17
  80.9 75.8 %collective-permute-done.2 = bf16[2,896,512]{2,1,0:T(8,128)(2,1)} collective-permute-done((bf16[2,896,512]{2,1,0:T(8,128)(2,1)}, bf16[2,896,512]{2,1,0:T(8,128)(2,1)}, u32[]{:S(2)}, u32[]{:S(2)}) %collective-permute-start.2) | collective-permute-done | bytes 1835040 | tf_op jit(solution)/shard_map/ppermute | solution.py:17
  156.7 40.3 %collective-permute-done.3 = bf16[2,896,512]{2,1,0:T(8,128)(2,1)} collective-permute-done((bf16[2,896,512]{2,1,0:T(8,128)(2,1)}, bf16[2,896,512]{2,1,0:T(8,128)(2,1)}, u32[]{:S(2)}, u32[]{:S(2)}) %collective-permute-start.3) | collective-permute-done | bytes 1835040 | tf_op jit(solution)/shard_map/ppermute | solution.py:17
  197.0 4.1 select_select_fusion
  201.2 15.4 %collective-permute-done = bf16[2,896,512]{2,1,0:T(8,128)(2,1)} collective-permute-done((bf16[2,896,512]{2,1,0:T(8,128)(2,1)}, bf16[2,896,512]{2,1,0:T(8,128)(2,1)}, u32[]{:S(2)}, u32[]{:S(2)}) %collective-permute-start) | collective-permute-done | bytes 1835040 | tf_op jit(solution)/shard_map/ppermute | solution.py:17
  216.6 2.3 broadcast_in_dim.65
  218.9 256.7 %while.15 = (s32[]{:T(128)}, bf16[896,2048]{1,0:T(8,128)(2,1)}, bf16[896,2048]{1,0:T(8,128)(2,1)}, bf16[896,512]{1,0:T(8,128)(2,1)S(1)}, pred[]{:T(512)}, /*inde...) while((s32[]{:T(128)}, bf16[896,2048]{1,0:T(8,128)(2,1)}, ...), condition=%wide.region_11.12_spmd, body=%wide.region_2.11_spmd.sunk | while | flops 1682139648 | bytes 55405464 | solution.py:103
  218.9 1.7 fusion.60
  224.8 1.6 fusion.61
  230.4 1.6 convolution_multiply_fusion.5
  234.9 1.7 fusion.60
  240.8 1.6 fusion.61
  246.4 1.6 convolution_multiply_fusion.5
  250.9 1.7 fusion.60
  256.8 1.6 fusion.61
  262.4 1.6 convolution_multiply_fusion.5
  266.9 1.7 fusion.60
  272.8 1.6 fusion.61
  278.4 1.6 convolution_multiply_fusion.5
  282.9 1.7 fusion.60
  288.8 1.6 fusion.61
  294.5 1.6 convolution_multiply_fusion.5
  299.0 1.7 fusion.60
  304.9 1.6 fusion.61
  310.5 1.6 convolution_multiply_fusion.5
  315.0 1.7 fusion.60
  320.9 1.6 fusion.61
  326.5 1.6 convolution_multiply_fusion.5
  331.0 1.7 fusion.60
  336.9 1.6 fusion.61
  342.5 1.6 convolution_multiply_fusion.5
  347.0 1.7 fusion.60
  352.9 1.6 fusion.61
  358.5 1.6 convolution_multiply_fusion.5
  363.1 1.7 fusion.60
  369.0 1.6 fusion.61
  374.6 1.6 convolution_multiply_fusion.5
  379.1 1.7 fusion.60
  385.0 1.6 fusion.61
  390.7 1.6 convolution_multiply_fusion.5
  395.2 1.7 fusion.60
  401.1 1.6 fusion.61
  406.7 1.6 convolution_multiply_fusion.5
  411.3 1.7 fusion.60
  417.2 1.6 fusion.61
  422.8 1.6 convolution_multiply_fusion.5
  427.3 1.7 fusion.60
  433.3 1.6 fusion.61
  438.9 1.6 convolution_multiply_fusion.5
  443.4 1.7 fusion.60
  455.0 1.6 convolution_multiply_fusion.5
  459.5 1.7 fusion.60
  471.0 1.6 convolution_multiply_fusion.5
  475.6 30.7 %all_to_all.77 = bf16[2,448,2048]{2,1,0:T(8,128)(2,1)S(1)} all-to-all(bf16[2,448,2048]{2,1,0:T(8,128)(2,1)} %bitcast.70), channel_id=1, replica_groups=mesh['seq'=16,'head'=2] {'head'}, dimensions={0} | all-to-all | bytes 7340032 | tf_op jit(solution)/shard_map/all_to_all | solution.py:106
  506.2 2.3 copy.20
  (196 shorter events, 186.1 us)
Async XLA Ops:
  0.0 5.8 %copy-start.3 = (bf16[448,1024]{1,0:T(8,128)(2,1)S(1)}, bf16[448,1024]{1,0:T(8,128)(2,1)}, u32[]{:S(2)}) copy-start(bf16[448,1024]{1,0:T(8,128)(2,1)} %param.9) | copy-start | bytes 2752516
  2.3 16.0 %all-to-all-start.1 = ((bf16[448,2,512]{2,0,1:T(8,128)(2,1)}), bf16[448,2,512]{2,0,1:T(8,128)(2,1)S(1)}, u32[]{:S(2)}, u32[]{:S(2)}) async-start(bf16[448,2,512]{2,0,1:T(8,128)(2,1)} %bitcast.55), calls=%async_computation.1 | async-start | bytes 1835008 | tf_op jit(solution)/shard_map/all_to_all | solution.py:53
  18.3 24.9 %copy-start.1 = (bf16[448,4096]{1,0:T(8,128)(2,1)S(1)}, bf16[448,4096]{1,0:T(8,128)(2,1)}, u32[]{:S(2)}) copy-start(bf16[448,4096]{1,0:T(8,128)(2,1)} %param.7) | copy-start | bytes 11010052
  32.6 0.9 copy-start
  34.9 45.9 %collective-permute-start.1 = (bf16[2,896,512]{2,1,0:T(8,128)(2,1)}, bf16[2,896,512]{2,1,0:T(8,128)(2,1)S(1)}, u32[]{:S(2)}, u32[]{:S(2)}) collective-permute-start(bf16[2,896,512]{2,1,0:T(8,128)(2,1)} %pad_maximum_fusion), channel_id=1, source_target_pairs={{0,16},{2,18},{4,20},{6,22},{8,24},{10,26},{12,28},{14,30},{1,17},... | collective-permute-start | bytes 5505032 | tf_op jit(solution)/shard_map/ppermute | solution.py:17
  36.2 120.5 %collective-permute-start.2 = (bf16[2,896,512]{2,1,0:T(8,128)(2,1)}, bf16[2,896,512]{2,1,0:T(8,128)(2,1)}, u32[]{:S(2)}, u32[]{:S(2)}) collective-permute-start(bf16[2,896,512]{2,1,0:T(8,128)(2,1)} %pad_maximum_fusion), channel_id=1, source_target_pairs={{0,8},{2,10},{4,12},{6,14},{8,16},{10,18},{12,20},{14,22},{16,24},... | collective-permute-start | bytes 5505032 | tf_op jit(solution)/shard_map/ppermute | solution.py:17
  39.7 157.3 %collective-permute-start.3 = (bf16[2,896,512]{2,1,0:T(8,128)(2,1)}, bf16[2,896,512]{2,1,0:T(8,128)(2,1)}, u32[]{:S(2)}, u32[]{:S(2)}) collective-permute-start(bf16[2,896,512]{2,1,0:T(8,128)(2,1)} %pad_maximum_fusion), channel_id=1, source_target_pairs={{0,4},{2,6},{4,8},{6,10},{8,12},{10,14},{12,16},{14,18},{16,20},{1... | collective-permute-start | bytes 5505032 | tf_op jit(solution)/shard_map/ppermute | solution.py:17
  45.4 7.5 %copy-start.4 = (s32[1,3]{1,0:T(1,128)S(1)}, s32[1,3]{1,0:T(1,128)}, u32[]{:S(2)}) copy-start(s32[1,3]{1,0:T(1,128)} %param.10) | copy-start | bytes 40
  45.4 9.9 %copy-start.5 = (s32[3]{0:T(128)S(1)}, s32[3]{0:T(128)}, u32[]{:S(2)}) copy-start(s32[3]{0:T(128)} %constant.171.clone) | copy-start | bytes 40
  45.4 155.7 %all-to-all-start = ((bf16[448,2,2048]{2,0,1:T(8,128)(2,1)}), bf16[448,2,2048]{2,0,1:T(8,128)(2,1)}, u32[]{:S(2)}, u32[]{:S(2)}) async-start(bf16[448,2,2048]{2,0,1:T(8,128)(2,1)} %bitcast.68), calls=%async_computation | async-start | bytes 7340032 | tf_op jit(solution)/shard_map/all_to_all | solution.py:52
  51.0 165.6 %collective-permute-start = (bf16[2,896,512]{2,1,0:T(8,128)(2,1)}, bf16[2,896,512]{2,1,0:T(8,128)(2,1)}, u32[]{:S(2)}, u32[]{:S(2)}) collective-permute-start(bf16[2,896,512]{2,1,0:T(8,128)(2,1)} %pad_maximum_fusion), channel_id=1, source_target_pairs={{0,2},{2,4},{4,6},{6,8},{8,10},{10,12},{12,14},{14,16},{16,18},{18... | collective-permute-start | bytes 5505032 | tf_op jit(solution)/shard_map/ppermute | solution.py:17
  80.9 75.8 %copy-start.2 = (bf16[2,896,512]{2,1,0:T(8,128)(2,1)}, bf16[2,896,512]{2,1,0:T(8,128)(2,1)S(1)}, u32[]{:S(2)}) copy-start(bf16[2,896,512]{2,1,0:T(8,128)(2,1)S(1)} %collective-permute-done.1) | copy-start | bytes 5505028
where the time goes:
time: 512 us; the launch traced here: 509 us
  matrix products  170 us (33%)
  waiting for transfers between devices  165 us (32%)
  local copies, waits for them, and re-layouts  63 us (12%)
  blocking collectives  45 us (9%)
  other arithmetic  39.6 us (8%)
  starting transfers between devices  19.2 us (4%)
  between operations  5.43 us (1%)
    ppermute x4, waiting for transfers between devices, passed_along(): return lax.ppermute(value, axis, pairs)  153 us
    dot_general x64, matrix products, block_terms(): lax.dot_general(query_head, key_head, (((1,), (1,)), ((), ())), preferred...  98.2 us
    dot_general x64, matrix products, block_terms(): jnp.dot(weights, value_head, preferred_element_type=jnp.float32)  71.9 us
    slice x32, local copies, waits for them, and re-layouts, one_head(): value_head = lax.dynamic_slice_in_dim(remote[1], offset, HEAD_SIZE, 1)  52.3 us
    reduce_sum x48, other arithmetic, block_terms(): row_total = jnp.sum(weights.astype(jnp.float32), axis=-1)  33 us
    all_to_all x1, blocking collectives, per_device(): lax.all_to_all(attended, 'head', split_axis=0, concat_axis=1, tiled=True)  30.7 us
    all_to_all x1, blocking collectives, per_device(): lax.all_to_all(input_values, 'head', split_axis=1, concat_axis=0, tiled=T...  14.3 us
    all_to_all x1, waiting for transfers between devices, per_device(): lax.all_to_all(encoded_keys, 'head', split_axis=1, concat_axis=0, tiled=T...  12.4 us
  transfers between devices with their start and end apart: 6, of which 5 were waited for; matrix products, arithmetic and copies ran while one was open for 2% of the time, Pallas kernels for 0%

commit v1 on v0

v1 whole, which is shorter than its diff:
```python
from functools import partial, reduce

import jax
import jax.numpy as jnp
from jax import lax
from jax.experimental import pallas as pl
from jax.experimental.pallas import tpu as pltpu
from jax.sharding import PartitionSpec as P

HEAD_SIZE = 128
LANES = 128
EXPONENT_SCALE = HEAD_SIZE ** (-0.5) * 1.4426950408889634
KEY_HEADS_PER_GROUP = 2

negative_fill = -1e30


def passed_along(value, axis, by):
    devices = lax.axis_size(axis)
    pairs = [(i, i + by) for i in range(devices) if 0 <= i + by < devices]
    return lax.ppermute(value, axis, pairs)


def swapped(value, axis, distance):
    devices = lax.axis_size(axis)
    return lax.ppermute(value, axis, [(i, i ^ distance) for i in range(devices)])


def gather_heads(arrays, offset, widths):
    count = lax.axis_size("head")
    share = [array.shape[1] // count for array in arrays]

    def columns(owner):
        return jnp.concatenate(
            [
                lax.dynamic_slice_in_dim(array, owner * s + offset * w, w, 1)
                for array, s, w in zip(arrays, share, widths)
            ],
            axis=1,
        )

    if count == 2:
        mine = lax.axis_index("head")
        kept = columns(mine)
        arrived = swapped(columns(1 - mine), "head", 1)
        return jnp.where(
            mine == 0,
            jnp.concatenate([kept, arrived], axis=0),
            jnp.concatenate([arrived, kept], axis=0),
        )
    whole = jnp.concatenate([columns(owner) for owner in range(count)], axis=1)
    return lax.all_to_all(whole, "head", split_axis=1, concat_axis=0, tiled=True)


def return_tokens(result):
    count = lax.axis_size("head")
    rows = result.shape[0] // count
    if count == 2:
        mine = lax.axis_index("head")
        kept = lax.dynamic_slice_in_dim(result, mine * rows, rows, 0)
        arrived = swapped(
            lax.dynamic_slice_in_dim(result, (1 - mine) * rows, rows, 0), "head", 1
        )
        return [jnp.where(mine == 0, kept, arrived), jnp.where(mine == 0, arrived, kept)]
    whole = lax.all_to_all(result, "head", split_axis=0, concat_axis=1, tiled=True)
    return jnp.split(whole, count, axis=1)


def attention_kernel(sharing, far_count, choice_ref, query_ref, *refs):
    keys = refs[: 2 + far_count]
    values = refs[2 + far_count : 2 * (2 + far_count)]
    out_ref, key_far, value_all, scores = refs[2 * (2 + far_count) :]
    length = query_ref.shape[0]
    half = length // 2
    near = -(-half // LANES) * LANES

    for block in range(2):
        value_all[block, :, :HEAD_SIZE] = values[block][...]
    value_all[:, :, HEAD_SIZE:] = jnp.ones((4, length, HEAD_SIZE), jnp.bfloat16)
    for column in range(2):
        for number in range(far_count):

            @pl.when(choice_ref[3 + column] == number)
            def _():
                key_far[column] = keys[2 + number][...]
                value_all[2 + column, :, :HEAD_SIZE] = values[2 + number][...]

    valid = [None] + [choice_ref[column] > 0 for column in range(3)]
    scale = [jnp.float32(EXPONENT_SCALE)] + [
        jnp.where(valid[block], EXPONENT_SCALE, 0.0) for block in range(1, 4)
    ]

    def widths(tile):
        return [near if tile == 0 else length, length, length, length]

    def score_block(head, tile, block):
        query = query_ref[
            pl.ds(tile * half, half), pl.ds(pl.multiple_of(head * HEAD_SIZE, HEAD_SIZE), HEAD_SIZE)
        ]
        width = widths(tile)[block]
        key = key_far[block - 2] if block >= 2 else keys[block][:width, :]
        result = lax.dot_general(
            query, key, (((1,), (1,)), ((), ())), preferred_element_type=jnp.float32
        )
        if block == 0:
            row = lax.broadcasted_iota(jnp.int32, result.shape, 0) + tile * half
            column = lax.broadcasted_iota(jnp.int32, result.shape, 1)
            result = jnp.where(column <= row, result, negative_fill)
        scores[tile, block, :, :width] = result
        partial_top = reduce(
            jnp.maximum, [result[:, i : i + LANES] for i in range(0, width, LANES)]
        )
        if block > 0:
            partial_top = jnp.where(valid[block], partial_top, negative_fill)
        return partial_top

    def weigh_block(tile, block, top):
        width = widths(tile)[block]
        shift = top * EXPONENT_SCALE
        if block > 0:
            shift = jnp.where(valid[block], shift, -negative_fill)
        weights = jnp.exp2(scores[tile, block, :, :width] * scale[block] - shift)
        return jnp.dot(
            weights.astype(jnp.bfloat16),
            value_all[block, :width, :],
            preferred_element_type=jnp.float32,
        )

    def top_of(partials):
        return jnp.max(reduce(jnp.maximum, partials), axis=1, keepdims=True)

    def stage(score_head, score_tile, weigh_head, weigh_tile, top):
        partials = []
        total = None
        for block in range(4):
            partials.append(score_block(score_head, score_tile, block))
            part = weigh_block(weigh_tile, block, top)
            total = part if total is None else total + part
        out_ref[
            pl.ds(weigh_tile * half, half),
            pl.ds(pl.multiple_of(weigh_head * HEAD_SIZE, HEAD_SIZE), HEAD_SIZE),
        ] = (total[:, :HEAD_SIZE] / total[:, HEAD_SIZE:]).astype(jnp.bfloat16)
        return top_of(partials)

    first = top_of([score_block(0, 0, block) for block in range(4)])

    def one_head(head, top):
        top = stage(head, 1, head, 0, top)
        return stage(jnp.minimum(head + 1, sharing - 1), 0, head, 1, top)

    lax.fori_loop(0, sharing, one_head, first)


def attention(choice, query, blocks):
    length, width = query.shape
    key_heads = blocks[0].shape[1] // (2 * HEAD_SIZE)
    group = width // key_heads
    query_spec = pl.BlockSpec((length, group), lambda i, *_: (0, i))
    key_spec = pl.BlockSpec((length, HEAD_SIZE), lambda i, *_: (0, i))
    value_spec = pl.BlockSpec((length, HEAD_SIZE), lambda i, *_: (0, i + key_heads))
    flops = 4 * 4 * length * length * width
    return pl.pallas_call(
        partial(attention_kernel, group // HEAD_SIZE, len(blocks) - 2),
        out_shape=jax.ShapeDtypeStruct((length, width), jnp.bfloat16),
        grid_spec=pltpu.PrefetchScalarGridSpec(
            num_scalar_prefetch=1,
            grid=(key_heads,),
            in_specs=[query_spec] + [key_spec] * len(blocks) + [value_spec] * len(blocks),
            out_specs=query_spec,
            scratch_shapes=[
                pltpu.VMEM((2, length, HEAD_SIZE), jnp.bfloat16),
                pltpu.VMEM((4, length, 2 * HEAD_SIZE), jnp.bfloat16),
                pltpu.VMEM((2, 4, length // 2, length), jnp.float32),
            ],
        ),
        cost_estimate=pl.CostEstimate(
            flops=flops, bytes_accessed=4 * length * width, transcendentals=flops // 512
        ),
        compiler_params=pltpu.CompilerParams(vmem_limit_bytes=56 * 1024 * 1024),
    )(choice, query, *blocks, *blocks)


def per_device(query_input, encoded_keys, input_values, sources):
    head_devices = lax.axis_size("head")
    span_count = lax.axis_size("seq")
    own_index = lax.axis_index("seq")
    key_heads = encoded_keys.shape[1] // HEAD_SIZE // head_devices
    sharing = query_input.shape[1] // encoded_keys.shape[1]
    distances = [2**power for power in range(1, 31) if 2**power < span_count]
    row = sources[0]
    distance_table = jnp.array(distances, jnp.int32)
    slots = [
        jnp.sum((distance_table < own_index - row[column]).astype(jnp.int32)) for column in (1, 2)
    ]
    choice = jnp.stack(
        [(row[column] >= 0).astype(jnp.int32) for column in range(3)]
        + [jnp.clip(slot, 0, len(distances) - 1) for slot in slots]
    )
    size = min(KEY_HEADS_PER_GROUP, key_heads)
    width = size * HEAD_SIZE
    pieces = [[] for _ in range(head_devices)]
    for number in range(key_heads // size):
        own = gather_heads([encoded_keys, input_values], number, [width, width])
        query = gather_heads([query_input], number, [width * sharing])
        far = {4: passed_along(own, "seq", 4)}
        far[2] = swapped(jnp.where(own_index // 2 % 2 == 0, own, far[4]), "seq", 2)
        far[1] = swapped(jnp.where(own_index % 2 == 0, own, far[2]), "seq", 1)
        for distance in distances[2:]:
            far[distance] = passed_along(far[distance // 2], "seq", distance // 2)
        result = attention(choice, query, [own, far[1]] + [far[d] for d in distances])
        for owner, piece in enumerate(return_tokens(result)):
            pieces[owner].append(piece)
    return jnp.concatenate([piece for owner in pieces for piece in owner], axis=1)


def solution(mesh):
    in_specs = (
        P(("seq", "head"), None),
        P(("seq", "head"), None),
        P(("seq", "head"), None),
        P("seq", None),
    )
    out_specs = P(("seq", "head"), None)
    return jax.shard_map(
        per_device, mesh=mesh, in_specs=in_specs, out_specs=out_specs, check_vma=False
    )
```

time: 512 us -> 205 us (0.40)
  matrix products: 170 us -> 0 us
  waiting for transfers between devices: 165 us -> 66.2 us
  Pallas kernels: 0 us -> 76.6 us
  local copies, waits for them, and re-layouts: 63 us -> 12 us
  blocking collectives: 45 us -> 0 us
  other arithmetic: 39.6 us -> 18.2 us
  starting transfers between devices: 19.2 us -> 25.2 us
    dot_general x128 -> x0, matrix products: 170 us -> none  [the longest x64 98.2 us: block_terms(): lax.dot_general(query_head, key_head, (((1,), (1,)), ((), ())), preferred...]
    ppermute x4, waiting for transfers between devices: 153 us -> 16.5 us  [passed_along(): return lax.ppermute(value, axis, pairs)]
    pallas_call x0 -> x2, Pallas kernels: none -> 76.6 us  [attention(): pl.pallas_call(partial(attention_kernel, group // HEAD_SIZE, len(blocks)...]
    slice x33 -> x1, local copies, waits for them, and re-layouts: 52.8 us -> 0.6 us  [per_device(): row[column] >= 0]
    ppermute x0 -> x10, waiting for transfers between devices: none -> 49.7 us  [swapped(): lax.ppermute(value, axis, [(i, i ^ distance) for i in range(devices)])]
    all_to_all x2 -> x0, blocking collectives: 45 us -> none  [the longest x1 30.7 us: per_device(): lax.all_to_all(attended, 'head', split_axis=0, concat_axis=1, tiled=True)]
    reduce_sum x49 -> x1, other arithmetic: 33.6 us -> 0.64 us  [per_device(): jnp.sum((distance_table < own_index - row[column]).astype(jnp.int32))]
    ppermute x0 -> x10, starting transfers between devices: none -> 12.7 us  [swapped(): lax.ppermute(value, axis, [(i, i ^ distance) for i in range(devices)])]
  transfers between devices with their start and end apart: 6 -> 14, of which waited for: 5 -> 6; matrix products, arithmetic and copies ran while one was open for 2% -> 11% of each run, Pallas kernels for 0% -> 38%
where the time goes in v1:
time: 205 us; the launch traced here: 203 us
  Pallas kernels  76.6 us (37%)
  waiting for transfers between devices  66.2 us (32%)
  starting transfers between devices  25.2 us (12%)
  other arithmetic  18.2 us (9%)
  local copies, waits for them, and re-layouts  12 us (6%)
  between operations  4.4 us (2%)
    pallas_call x2, Pallas kernels, attention(): pl.pallas_call(partial(attention_kernel, group // HEAD_SIZE, len(blocks)...  76.6 us
    ppermute x10, waiting for transfers between devices, swapped(): lax.ppermute(value, axis, [(i, i ^ distance) for i in range(devices)])  49.7 us
    ppermute x4, waiting for transfers between devices, passed_along(): return lax.ppermute(value, axis, pairs)  16.5 us
    ppermute x10, starting transfers between devices, swapped(): lax.ppermute(value, axis, [(i, i ^ distance) for i in range(devices)])  12.7 us
    ppermute x4, starting transfers between devices, passed_along(): return lax.ppermute(value, axis, pairs)  12.5 us
    select_n x4, other arithmetic, gather_heads(): jnp.where(mine == 0, jnp.concatenate([kept, arrived], axis=0), jnp.concat...  8.86 us
    dynamic_slice x2, local copies, waits for them, and re-layouts, columns(): lax.dynamic_slice_in_dim(array, owner * s + offset * w, w, 1)  5.33 us
  transfers between devices with their start and end apart: 14, of which 6 were waited for; matrix products, arithmetic and copies ran while one was open for 11% of the time, Pallas kernels for 38%

profile of v1, /device:TPU:16, one launch (start us, length us, event | category | flops | bytes accessed | tf_op | source)
XLA Modules:
  0.0 202.7 jit_solution(10628657078673116342)
XLA Ops:
  0.0 1.7 constant_dynamic-slice_fusion.10
  1.7 1.6 collective-permute-start.1
  3.3 10.7 %collective-permute-done.1 = bf16[448,512]{1,0:T(8,128)(2,1)S(1)} collective-permute-done((bf16[448,512]{1,0:T(8,128)(2,1)S(1)}, bf16[448,512]{1,0:T(8,128)(2,1)S(1)}, u32[]{:S(2)}, u32[]{:S(2)}) %collective-permute-start.1) | collective-permute-done | bytes 458784 | tf_op jit(solution)/shard_map/ppermute | solution.py:26
  14.1 0.4 maximum_select_fusion.2.refs_0_.refs_5_
  14.5 0.0 copy-start
  14.5 3.5 %collective-permute-start.2 = (bf16[896,512]{1,0:T(8,128)(2,1)S(1)}, bf16[896,512]{1,0:T(8,128)(2,1)}, u32[]{:S(2)}, u32[]{:S(2)}) collective-permute-start(bf16[896,512]{1,0:T(8,128)(2,1)S(1)} %maximum_select_fusion.2.refs_0_.refs_5_), channel_id=1, source_target_pairs={{0,8},{2,10},{4,12},{6,14},{8,16},{10,18},{12,20},{14,22},{16,24},... | collective-permute-start | bytes 2752520 | tf_op jit(solution)/shard_map/ppermute | solution.py:21
  18.0 1.6 collective-permute-start.8
  19.6 9.6 %collective-permute-done.8 = bf16[448,512]{1,0:T(8,128)(2,1)S(1)} collective-permute-done((bf16[448,512]{1,0:T(8,128)(2,1)S(1)}, bf16[448,512]{1,0:T(8,128)(2,1)S(1)}, u32[]{:S(2)}, u32[]{:S(2)}) %collective-permute-start.8) | collective-permute-done | bytes 458784 | tf_op jit(solution)/shard_map/ppermute | solution.py:26
  29.2 0.4 maximum_select_fusion.3.refs_0_.refs_5_
  29.6 0.0 copy-start.1
  29.6 1.9 collective-permute-start.9
  31.5 8.2 %collective-permute-done.2.refs_3_.refs_8_ = bf16[896,512]{1,0:T(8,128)(2,1)} collective-permute-done((bf16[896,512]{1,0:T(8,128)(2,1)S(1)}, bf16[896,512]{1,0:T(8,128)(2,1)}, u32[]{:S(2)}, u32[]{:S(2)}) %collective-permute-start.2) | collective-permute-done | bytes 917536 | tf_op jit(solution)/shard_map/ppermute | solution.py:21
  39.8 1.0 broadcast_select_fusion.1
  40.8 2.7 %collective-permute-start.3 = (bf16[896,512]{1,0:T(8,128)(2,1)}, bf16[896,512]{1,0:T(8,128)(2,1)}, u32[]{:S(2)}, u32[]{:S(2)}) collective-permute-start(bf16[896,512]{1,0:T(8,128)(2,1)} %broadcast_select_fusion.1), channel_id=1, source_target_pairs={{0,4},{2,6},{4,0},{6,2},{8,12},{10,14},{12,8},{14,10},{16,20},{18,... | collective-permute-start | bytes 2752520 | tf_op jit(solution)/shard_map/ppermute | solution.py:26
  43.4 3.6 %constant_dynamic-slice_fusion.13 = (bf16[448,1024]{1,0:T(8,128)(2,1)}, bf16[448,1024]{1,0:T(8,128)(2,1)}, bf16[448,1024]{1,0:T(8,128)(2,1)}, bf16[448,1024]{1,0:T(8,128)(2,1)S(1)}) fusion(bf16[448,4096]{1,0:T(8,128)(2,1)} %param.5, s32[]{:T(128)S(6)} %select_n.122, s32[]{:T(128)S(6)} %select_n.123, s32[]{:T(128)S(6)} %select_n.140, s32[]{:T(128)S(6)} %select_n.139), kind=kLoop, calls=%fused_computation.28 | loop fusion | bytes 7340048 | tf_op jit(solution)/shard_map/dynamic_slice | solution.py:36
  47.1 1.5 collective-permute-start
  48.6 0.5 collective-permute-start.7
  49.1 8.3 %collective-permute-done.9.refs_3_.refs_8_ = bf16[896,512]{1,0:T(8,128)(2,1)} collective-permute-done((bf16[896,512]{1,0:T(8,128)(2,1)S(1)}, bf16[896,512]{1,0:T(8,128)(2,1)}, u32[]{:S(2)}, u32[]{:S(2)}) %collective-permute-start.9) | collective-permute-done | bytes 917536 | tf_op jit(solution)/shard_map/ppermute | solution.py:21
  57.3 1.0 broadcast_select_fusion
  58.4 0.0 copy-start.4
  58.4 0.0 copy-start.5
  58.4 2.7 %collective-permute-start.10 = (bf16[896,512]{1,0:T(8,128)(2,1)}, bf16[896,512]{1,0:T(8,128)(2,1)}, u32[]{:S(2)}, u32[]{:S(2)}) collective-permute-start(bf16[896,512]{1,0:T(8,128)(2,1)} %broadcast_select_fusion), channel_id=1, source_target_pairs={{0,4},{2,6},{4,0},{6,2},{8,12},{10,14},{12,8},{14,10},{16,20},{18,... | collective-permute-start | bytes 2752520 | tf_op jit(solution)/shard_map/ppermute | solution.py:26
  61.0 3.5 %collective-permute-start.5 = (bf16[896,512]{1,0:T(8,128)(2,1)}, bf16[896,512]{1,0:T(8,128)(2,1)}, u32[]{:S(2)}, u32[]{:S(2)}) collective-permute-start(bf16[896,512]{1,0:T(8,128)(2,1)} %collective-permute-done.2.refs_3_.refs_8_), channel_id=1, source_target_pairs={{0,8},{2,10},{4,12},{6,14},{8,16},{10,18},{12,20},{14,22},{16,24},... | collective-permute-start | bytes 2752520 | tf_op jit(solution)/shard_map/ppermute | solution.py:21
  64.5 0.0 collective-permute-done.3.refs_2_.refs_7_
  64.5 0.0 copy-done
  64.5 1.0 broadcast_select_fusion.3
  65.6 0.0 collective-permute-start.4
  65.6 0.0 copy-done.4
  65.6 0.6 fusion.2
  68.5 0.0 copy-done.5
  68.5 0.6 fusion.1
  71.1 0.6 stack.35.choice_ref
  71.6 0.0 collective-permute-done
  71.6 4.5 %maximum_select_fusion.query_ref = bf16[896,1024]{1,0:T(8,128)(2,1)} fusion(bf16[448,1024]{1,0:T(8,128)(2,1)} %collective-permute-done, bf16[448,1024]{1,0:T(8,128)(2,1)} %get-tuple-element.7, pred[]{:T(512)S(6)} %eq.11), kind=kLoop, calls=%fused_computation.1 | loop fusion | flops 8257536 | bytes 3670017 | tf_op jit(solution)/shard_map/jit(_where)/select_n | solution.py:46
  76.1 8.9 %collective-permute-done.7 = bf16[448,1024]{1,0:T(8,128)(2,1)} collective-permute-done((bf16[448,1024]{1,0:T(8,128)(2,1)}, bf16[448,1024]{1,0:T(8,128)(2,1)}, u32[]{:S(2)}, u32[]{:S(2)}) %collective-permute-start.7) | collective-permute-done | bytes 917536 | tf_op jit(solution)/shard_map/ppermute | solution.py:26
  85.0 3.6 %maximum_select_fusion.1.query_ref = bf16[896,1024]{1,0:T(8,128)(2,1)} fusion(bf16[448,1024]{1,0:T(8,128)(2,1)} %collective-permute-done.7, bf16[448,1024]{1,0:T(8,128)(2,1)S(1)} %get-tuple-element.10, pred[]{:T(512)S(6)} %eq.11), kind=kLoop, calls=%fused_computation.2 | loop fusion | flops 8257536 | bytes 3670017 | tf_op jit(solution)/shard_map/jit(_where)/select_n | solution.py:46
  88.6 3.7 %collective-permute-start.12 = (bf16[896,512]{1,0:T(8,128)(2,1)}, bf16[896,512]{1,0:T(8,128)(2,1)S(1)}, u32[]{:S(2)}, u32[]{:S(2)}) collective-permute-start(bf16[896,512]{1,0:T(8,128)(2,1)} %collective-permute-done.9.refs_3_.refs_8_), channel_id=1, source_target_pairs={{0,8},{2,10},{4,12},{6,14},{8,16},{10,18},{12,20},{14,22},{16,24},... | collective-permute-start | bytes 2752520 | tf_op jit(solution)/shard_map/ppermute | solution.py:21
  92.3 0.0 collective-permute-done.10.refs_2_.refs_7_
  92.3 0.0 copy-done.1
  92.3 0.1 broadcast_select_fusion.2
  92.4 0.1 collective-permute-start.11
  92.5 0.0 collective-permute-done.5.refs_4_.refs_9_
  92.5 0.0 collective-permute-done.4.refs_1_.refs_6_
  92.5 38.3 %shard_map.55 = bf16[896,1024]{1,0:T(8,128)(2,1)} custom-call(s32[5]{0:T(128)} %stack.35.choice_ref, bf16[896,1024]{1,0:T(8,128)(2,1)} %maximum_select_fusion.query_ref, bf16[896,512]{1,0:T(8,128)(2,1)} %copy-done, bf16[896,512]{1,0:T(8,128)(2,1)} %collective-permute-done.4.refs_1_.refs_6_, bf16[896,512]{1,0:T(8,128)(2,1)} %collective-permute-done.3.refs_2_.refs_7_, ...), custom_call_target="tpu_custom_call" | custom-call | flops 13153337344 | bytes 3670016 | tf_op jit(solution)/shard_map/pallas_call | solution.py:162
  130.8 1.2 constant_dynamic-slice_fusion.7
  132.1 1.6 collective-permute-start.6
  133.7 0.0 collective-permute-done.12.refs_4_.refs_9_
  133.7 0.0 copy-start.6
  133.7 0.0 collective-permute-done.11.refs_1_.refs_6_
  133.7 1.0 copy-done.6
  134.7 0.0 copy-start.7
  134.7 1.0 copy-done.7
  135.6 38.3 %shard_map.56 = bf16[896,1024]{1,0:T(8,128)(2,1)} custom-call(s32[5]{0:T(128)} %stack.35.choice_ref, bf16[896,1024]{1,0:T(8,128)(2,1)} %maximum_select_fusion.1.query_ref, bf16[896,512]{1,0:T(8,128)(2,1)} %copy-done.1, bf16[896,512]{1,0:T(8,128)(2,1)} %copy-done.7, bf16[896,512]{1,0:T(8,128)(2,1)} %collective-permute-done.10.refs_2_.refs_7_, ...), custom_call_target="tpu_custom_call" | custom-call | flops 13153337344 | bytes 3670016 | tf_op jit(solution)/shard_map/pallas_call | solution.py:162
  173.9 0.0 copy-start.2
  173.9 2.3 %constant_dynamic-slice_fusion = bf16[448,1024]{1,0:T(8,128)(2,1)} fusion(bf16[896,1024]{1,0:T(8,128)(2,1)} %shard_map.56, s32[]{:T(128)S(6)} %select_n.137), kind=kLoop, calls=%fused_computation.15 | loop fusion | bytes 1835012 | tf_op jit(solution)/shard_map/dynamic_slice | solution.py:62
  176.2 0.5 collective-permute-start.13
  176.7 0.0 copy-start.3
  176.7 0.0 collective-permute-done.6
  176.7 0.0 copy-done.2
  176.7 1.8 broadcast_select_fusion.7
  178.5 20.4 %collective-permute-done.13 = bf16[448,1024]{1,0:T(8,128)(2,1)} collective-permute-done((bf16[448,1024]{1,0:T(8,128)(2,1)}, bf16[448,1024]{1,0:T(8,128)(2,1)}, u32[]{:S(2)}, u32[]{:S(2)}) %collective-permute-start.13) | collective-permute-done | bytes 917536 | tf_op jit(solution)/shard_map/ppermute | solution.py:26
  199.0 0.0 copy-done.3
  199.0 1.7 broadcast_select_fusion.6
  200.6 2.0 pad_maximum_fusion
  (2 shorter events, 0.1 us)
Async XLA Ops:
  1.7 12.3 %collective-permute-start.1 = (bf16[448,512]{1,0:T(8,128)(2,1)S(1)}, bf16[448,512]{1,0:T(8,128)(2,1)S(1)}, u32[]{:S(2)}, u32[]{:S(2)}) collective-permute-start(bf16[448,512]{1,0:T(8,128)(2,1)S(1)} %pad_maximum_fusion.1), channel_id=1, source_target_pairs={{0,1},{1,0},{2,3},{3,2},{4,5},{5,4},{6,7},{7,6},{8,9},{9,8},{10,11... | collective-permute-start | bytes 1376264 | tf_op jit(solution)/shard_map/ppermute | solution.py:26
  14.5 50.1 %copy-start = (bf16[896,512]{1,0:T(8,128)(2,1)}, bf16[896,512]{1,0:T(8,128)(2,1)S(1)}, u32[]{:S(2)}) copy-start(bf16[896,512]{1,0:T(8,128)(2,1)S(1)} %maximum_select_fusion.2.refs_0_.refs_5_) | copy-start | bytes 2752516
  14.5 25.3 %collective-permute-start.2 = (bf16[896,512]{1,0:T(8,128)(2,1)S(1)}, bf16[896,512]{1,0:T(8,128)(2,1)}, u32[]{:S(2)}, u32[]{:S(2)}) collective-permute-start(bf16[896,512]{1,0:T(8,128)(2,1)S(1)} %maximum_select_fusion.2.refs_0_.refs_5_), channel_id=1, source_target_pairs={{0,8},{2,10},{4,12},{6,14},{8,16},{10,18},{12,20},{14,22},{16,24},... | collective-permute-start | bytes 2752520 | tf_op jit(solution)/shard_map/ppermute | solution.py:21
  18.0 11.2 %collective-permute-start.8 = (bf16[448,512]{1,0:T(8,128)(2,1)S(1)}, bf16[448,512]{1,0:T(8,128)(2,1)S(1)}, u32[]{:S(2)}, u32[]{:S(2)}) collective-permute-start(bf16[448,512]{1,0:T(8,128)(2,1)S(1)} %pad_maximum_fusion.2), channel_id=1, source_target_pairs={{0,1},{1,0},{2,3},{3,2},{4,5},{5,4},{6,7},{7,6},{8,9},{9,8},{10,11... | collective-permute-start | bytes 1376264 | tf_op jit(solution)/shard_map/ppermute | solution.py:26
  29.6 62.7 %copy-start.1 = (bf16[896,512]{1,0:T(8,128)(2,1)}, bf16[896,512]{1,0:T(8,128)(2,1)S(1)}, u32[]{:S(2)}) copy-start(bf16[896,512]{1,0:T(8,128)(2,1)S(1)} %maximum_select_fusion.3.refs_0_.refs_5_) | copy-start | bytes 2752516
  29.6 27.8 %collective-permute-start.9 = (bf16[896,512]{1,0:T(8,128)(2,1)S(1)}, bf16[896,512]{1,0:T(8,128)(2,1)}, u32[]{:S(2)}, u32[]{:S(2)}) collective-permute-start(bf16[896,512]{1,0:T(8,128)(2,1)S(1)} %maximum_select_fusion.3.refs_0_.refs_5_), channel_id=1, source_target_pairs={{0,8},{2,10},{4,12},{6,14},{8,16},{10,18},{12,20},{14,22},{16,24},... | collective-permute-start | bytes 2752520 | tf_op jit(solution)/shard_map/ppermute | solution.py:21
  40.8 23.8 %collective-permute-start.3 = (bf16[896,512]{1,0:T(8,128)(2,1)}, bf16[896,512]{1,0:T(8,128)(2,1)}, u32[]{:S(2)}, u32[]{:S(2)}) collective-permute-start(bf16[896,512]{1,0:T(8,128)(2,1)} %broadcast_select_fusion.1), channel_id=1, source_target_pairs={{0,4},{2,6},{4,0},{6,2},{8,12},{10,14},{12,8},{14,10},{16,20},{18,... | collective-permute-start | bytes 2752520 | tf_op jit(solution)/shard_map/ppermute | solution.py:26
  47.1 24.6 %collective-permute-start = (bf16[448,1024]{1,0:T(8,128)(2,1)}, bf16[448,1024]{1,0:T(8,128)(2,1)}, u32[]{:S(2)}, u32[]{:S(2)}) collective-permute-start(bf16[448,1024]{1,0:T(8,128)(2,1)} %get-tuple-element.8), channel_id=1, source_target_pairs={{0,1},{1,0},{2,3},{3,2},{4,5},{5,4},{6,7},{7,6},{8,9},{9,8},{10,11... | collective-permute-start | bytes 2752520 | tf_op jit(solution)/shard_map/ppermute | solution.py:26
  48.6 36.4 %collective-permute-start.7 = (bf16[448,1024]{1,0:T(8,128)(2,1)}, bf16[448,1024]{1,0:T(8,128)(2,1)}, u32[]{:S(2)}, u32[]{:S(2)}) collective-permute-start(bf16[448,1024]{1,0:T(8,128)(2,1)} %get-tuple-element.9), channel_id=1, source_target_pairs={{0,1},{1,0},{2,3},{3,2},{4,5},{5,4},{6,7},{7,6},{8,9},{9,8},{10,11... | collective-permute-start | bytes 2752520 | tf_op jit(solution)/shard_map/ppermute | solution.py:26
  58.4 7.2 %copy-start.4 = (s32[1,3]{1,0:T(1,128)S(1)}, s32[1,3]{1,0:T(1,128)}, u32[]{:S(2)}) copy-start(s32[1,3]{1,0:T(1,128)} %param.8) | copy-start | bytes 40
  58.4 10.2 %copy-start.5 = (s32[3]{0:T(128)S(1)}, s32[3]{0:T(128)}, u32[]{:S(2)}) copy-start(s32[3]{0:T(128)} %constant.68.clone) | copy-start | bytes 40
  58.4 33.9 %collective-permute-start.10 = (bf16[896,512]{1,0:T(8,128)(2,1)}, bf16[896,512]{1,0:T(8,128)(2,1)}, u32[]{:S(2)}, u32[]{:S(2)}) collective-permute-start(bf16[896,512]{1,0:T(8,128)(2,1)} %broadcast_select_fusion), channel_id=1, source_target_pairs={{0,4},{2,6},{4,0},{6,2},{8,12},{10,14},{12,8},{14,10},{16,20},{18,... | collective-permute-start | bytes 2752520 | tf_op jit(solution)/shard_map/ppermute | solution.py:26
  61.0 31.4 %collective-permute-start.5 = (bf16[896,512]{1,0:T(8,128)(2,1)}, bf16[896,512]{1,0:T(8,128)(2,1)}, u32[]{:S(2)}, u32[]{:S(2)}) collective-permute-start(bf16[896,512]{1,0:T(8,128)(2,1)} %collective-permute-done.2.refs_3_.refs_8_), channel_id=1, source_target_pairs={{0,8},{2,10},{4,12},{6,14},{8,16},{10,18},{12,20},{14,22},{16,24},... | collective-permute-start | bytes 2752520 | tf_op jit(solution)/shard_map/ppermute | solution.py:21
  65.6 26.9 %collective-permute-start.4 = (bf16[896,512]{1,0:T(8,128)(2,1)}, bf16[896,512]{1,0:T(8,128)(2,1)}, u32[]{:S(2)}, u32[]{:S(2)}) collective-permute-start(bf16[896,512]{1,0:T(8,128)(2,1)} %broadcast_select_fusion.3), channel_id=1, source_target_pairs={{0,2},{2,0},{4,6},{6,4},{8,10},{10,8},{12,14},{14,12},{16,18},{18,... | collective-permute-start | bytes 2752520 | tf_op jit(solution)/shard_map/ppermute | solution.py:26
  88.6 45.0 %collective-permute-start.12 = (bf16[896,512]{1,0:T(8,128)(2,1)}, bf16[896,512]{1,0:T(8,128)(2,1)S(1)}, u32[]{:S(2)}, u32[]{:S(2)}) collective-permute-start(bf16[896,512]{1,0:T(8,128)(2,1)} %collective-permute-done.9.refs_3_.refs_8_), channel_id=1, source_target_pairs={{0,8},{2,10},{4,12},{6,14},{8,16},{10,18},{12,20},{14,22},{16,24},... | collective-permute-start | bytes 2752520 | tf_op jit(solution)/shard_map/ppermute | solution.py:21
  92.4 41.3 %collective-permute-start.11 = (bf16[896,512]{1,0:T(8,128)(2,1)S(1)}, bf16[896,512]{1,0:T(8,128)(2,1)S(1)}, u32[]{:S(2)}, u32[]{:S(2)}) collective-permute-start(bf16[896,512]{1,0:T(8,128)(2,1)S(1)} %broadcast_select_fusion.2), channel_id=1, source_target_pairs={{0,2},{2,0},{4,6},{6,4},{8,10},{10,8},{12,14},{14,12},{16,18},{18,... | collective-permute-start | bytes 2752520 | tf_op jit(solution)/shard_map/ppermute | solution.py:26
  132.1 44.7 %collective-permute-start.6 = (bf16[448,1024]{1,0:T(8,128)(2,1)S(1)}, bf16[448,1024]{1,0:T(8,128)(2,1)}, u32[]{:S(2)}, u32[]{:S(2)}) collective-permute-start(bf16[448,1024]{1,0:T(8,128)(2,1)S(1)} %constant_dynamic-slice_fusion.7), channel_id=1, source_target_pairs={{0,1},{1,0},{2,3},{3,2},{4,5},{5,4},{6,7},{7,6},{8,9},{9,8},{10,11... | collective-permute-start | bytes 2752520 | tf_op jit(solution)/shard_map/ppermute | solution.py:26
  133.7 1.0 copy-start.6
  134.7 1.0 copy-start.7
  173.9 2.8 %copy-start.2 = (bf16[896,1024]{1,0:T(8,128)(2,1)S(1)}, bf16[896,1024]{1,0:T(8,128)(2,1)}, u32[]{:S(2)}) copy-start(bf16[896,1024]{1,0:T(8,128)(2,1)} %shard_map.55) | copy-start | bytes 5505028
  176.2 22.8 %collective-permute-start.13 = (bf16[448,1024]{1,0:T(8,128)(2,1)}, bf16[448,1024]{1,0:T(8,128)(2,1)}, u32[]{:S(2)}, u32[]{:S(2)}) collective-permute-start(bf16[448,1024]{1,0:T(8,128)(2,1)} %constant_dynamic-slice_fusion), channel_id=1, source_target_pairs={{0,1},{1,0},{2,3},{3,2},{4,5},{5,4},{6,7},{7,6},{8,9},{9,8},{10,11... | collective-permute-start | bytes 2752520 | tf_op jit(solution)/shard_map/ppermute | solution.py:26
  176.7 22.3 %copy-start.3 = (bf16[896,1024]{1,0:T(8,128)(2,1)S(1)}, bf16[896,1024]{1,0:T(8,128)(2,1)}, u32[]{:S(2)}) copy-start(bf16[896,1024]{1,0:T(8,128)(2,1)} %shard_map.56) | copy-start | bytes 5505028

commit v2 on v1

--- a/solution.py
+++ b/solution.py
@@ -11,6 +11,9 @@
 LANES = 128
 EXPONENT_SCALE = HEAD_SIZE ** (-0.5) * 1.4426950408889634
 KEY_HEADS_PER_GROUP = 2
+
+MESH = pl.DeviceIdType.MESH
+OWN, ONE, TWO, FOUR, EIGHT = range(5)
 
 negative_fill = -1e30
 
@@ -180,6 +183,382 @@
     )(choice, query, *blocks, *blocks)
 
 
+def fused_kernel(
+    spans, choice_ref, query_ref, key_ref, value_ref, out_ref,
+    kv, query_all, result, key_far, value_all, scores,
+    local_q, local_kv, send_q, recv_q, send_kv, recv_kv,
+    send_four, recv_four, send_chain, recv_chain, local_out, send_out, recv_out,
+):
+    rows = query_ref.shape[0]
+    length = 2 * rows
+    groups = kv.shape[1]
+    heads = query_all.shape[2] // HEAD_SIZE
+    sharing = heads // groups
+    near = -(-rows // LANES) * LANES
+    span, mine = lax.axis_index("seq"), lax.axis_index("head")
+    other = 1 - mine
+    odd, odd_pair = span % 2, span // 2 % 2
+    beside = span + 1 - 2 * odd
+    across = span + 2 - 4 * odd_pair
+    has_before, has_after = span >= 4, span < spans - 4
+
+    barrier = pltpu.get_barrier_semaphore()
+    for device in ((span, other), (beside, mine), (across, mine)):
+        pl.semaphore_signal(barrier, inc=1, device_id=device, device_id_type=MESH)
+
+    @pl.when(has_before)
+    def _():
+        pl.semaphore_signal(barrier, inc=1, device_id=(span - 4, mine), device_id_type=MESH)
+
+    @pl.when(has_after)
+    def _():
+        pl.semaphore_signal(barrier, inc=1, device_id=(span + 4, mine), device_id_type=MESH)
+
+    def columns(start, count):
+        return pl.ds(pl.multiple_of(start * HEAD_SIZE, HEAD_SIZE), count * HEAD_SIZE)
+
+    def part(index):
+        return pl.ds(pl.multiple_of(index * rows, rows), rows)
+
+    def remote(source, target, send, receive, device):
+        return pltpu.make_async_remote_copy(
+            src_ref=source, dst_ref=target, send_sem=send, recv_sem=receive,
+            device_id=device, device_id_type=MESH,
+        )
+
+    def kv_local(group, which):
+        return pltpu.make_async_copy(
+            (key_ref, value_ref)[which].at[:, columns(mine * groups + group, 1)],
+            kv.at[OWN, group, which, part(mine), :],
+            local_kv.at[group, which],
+        )
+
+    def kv_swap(group, which):
+        return remote(
+            (key_ref, value_ref)[which].at[:, columns(other * groups + group, 1)],
+            kv.at[OWN, group, which, part(mine), :],
+            send_kv.at[group, which], recv_kv.at[group, which], (span, other),
+        )
+
+    def query_local(group):
+        return pltpu.make_async_copy(
+            query_ref.at[:, columns(mine * heads + group * sharing, sharing)],
+            query_all.at[mine, :, columns(group * sharing, sharing)],
+            local_q.at[group],
+        )
+
+    def query_swap(group):
+        return remote(
+            query_ref.at[:, columns(other * heads + group * sharing, sharing)],
+            query_all.at[mine, :, columns(group * sharing, sharing)],
+            send_q.at[group], recv_q.at[group], (span, other),
+        )
+
+    def four(group, step):
+        rows_part = part(mine) if step == 0 else part(other)
+        return remote(
+            kv.at[OWN, group, :, rows_part, :], kv.at[FOUR, group, :, rows_part, :],
+            send_four.at[group, step], recv_four.at[group, step], (span + 4, mine),
+        )
+
+    def chain(group, slot):
+        source, device = {
+            EIGHT: (FOUR, (span + 4, mine)),
+            TWO: (FOUR * odd_pair, (across, mine)),
+            ONE: (TWO * odd, (beside, mine)),
+        }[slot]
+        index = {ONE: 0, TWO: 1, EIGHT: 2}[slot]
+        return remote(
+            kv.at[source, group], kv.at[slot, group],
+            send_chain.at[group, index], recv_chain.at[group, index], device,
+        )
+
+    def out_local(head):
+        return pltpu.make_async_copy(
+            result.at[mine, :, columns(head, 1)],
+            out_ref.at[:, columns(mine * heads + head, 1)],
+            local_out.at[head],
+        )
+
+    def out_swap(head):
+        return remote(
+            result.at[other, :, columns(head, 1)],
+            out_ref.at[:, columns(mine * heads + head, 1)],
+            send_out.at[head], recv_out.at[head], (span, other),
+        )
+
+    def start_kv(group):
+        for which in range(2):
+            kv_swap(group, which).start()
+
+    def wait_kv(group):
+        for which in range(2):
+            kv_swap(group, which).wait_recv()
+
+    def start_four(group, step):
+        @pl.when(has_after)
+        def _():
+            four(group, step).start()
+
+    def wait_four(group):
+        @pl.when(has_before)
+        def _():
+            four(group, 0).wait_recv()
+            four(group, 1).wait_recv()
+
+    def start_eight(group):
+        @pl.when(jnp.logical_and(has_before, has_after))
+        def _():
+            chain(group, EIGHT).start()
+
+    def wait_eight(group):
+        @pl.when(span >= 8)
+        def _():
+            chain(group, EIGHT).wait_recv()
+
+    valid = [None] + [choice_ref[column] > 0 for column in range(3)]
+    scale = [jnp.float32(EXPONENT_SCALE)] + [
+        jnp.where(valid[block], EXPONENT_SCALE, 0.0) for block in range(1, 4)
+    ]
+
+    def prepare(group):
+        side = group % 2
+        for block in range(2):
+            value_all[side, block, :, :HEAD_SIZE] = kv[block, group, 1]
+        for column in range(2):
+            pick = choice_ref[3 + column]
+            for which in range(2):
+                chosen = lax.select(pick == 1, kv[FOUR, group, which], kv[TWO, group, which])
+                chosen = lax.select(pick == 2, kv[EIGHT, group, which], chosen)
+                if which == 0:
+                    key_far[side, column] = chosen
+                else:
+                    value_all[side, 2 + column, :, :HEAD_SIZE] = chosen
+
+    def widths(tile):
+        return [near if tile == 0 else length, length, length, length]
+
+    def score_block(head, tile, block):
+        group = head // sharing
+        query = query_all[tile, :, columns(head, 1)]
+        width = widths(tile)[block]
+        key = key_far[group % 2, block - 2] if block >= 2 else kv[block, group, 0, :width, :]
+        scored = lax.dot_general(
+            query, key, (((1,), (1,)), ((), ())), preferred_element_type=jnp.float32
+        )
+        if block == 0:
+            row = lax.broadcasted_iota(jnp.int32, scored.shape, 0) + tile * rows
+            column = lax.broadcasted_iota(jnp.int32, scored.shape, 1)
+            scored = jnp.where(column <= row, scored, negative_fill)
+        scores[tile, block, :, :width] = scored
+        partial_top = reduce(
+            jnp.maximum, [scored[:, i : i + LANES] for i in range(0, width, LANES)]
+        )
+        if block > 0:
+            partial_top = jnp.where(valid[block], partial_top, negative_fill)
+        return partial_top
+
+    def weigh_block(head, tile, block, top):
+        width = widths(tile)[block]
+        shift = top * EXPONENT_SCALE
+        if block > 0:
+            shift = jnp.where(valid[block], shift, -negative_fill)
+        weights = jnp.exp2(scores[tile, block, :, :width] * scale[block] - shift)
+        return jnp.dot(
+            weights.astype(jnp.bfloat16),
+            value_all[head // sharing % 2, block, :width, :],
+            preferred_element_type=jnp.float32,
+        )
+
+    def top_of(partials):
+        return jnp.max(reduce(jnp.maximum, partials), axis=1, keepdims=True)
+
+    def stage(score_head, score_tile, weigh_head, weigh_tile, top):
+        partials = []
+        total = None
+        for block in range(4):
+            partials.append(score_block(score_head, score_tile, block))
+            term = weigh_block(weigh_head, weigh_tile, block, top)
+            total = term if total is None else total + term
+        result[weigh_tile, :, columns(weigh_head, 1)] = (
+            total[:, :HEAD_SIZE] / total[:, HEAD_SIZE:]
+        ).astype(jnp.bfloat16)
+        return top_of(partials)
+
+    for group in range(groups):
+        for which in range(2):
+            kv_local(group, which).start()
+    for group in range(groups):
+        query_local(group).start()
+
+    pl.semaphore_wait(
+        barrier, 3 + jnp.where(has_before, 1, 0) + jnp.where(has_after, 1, 0)
+    )
+    start_kv(0)
+    for side in range(2):
+        value_all[side, :, :, HEAD_SIZE:] = jnp.ones((4, length, HEAD_SIZE), jnp.bfloat16)
+
+    @pl.when(jnp.logical_not(has_before))
+    def _():
+        for group in range(groups):
+            kv[FOUR, group] = jnp.zeros(kv.shape[2:], jnp.bfloat16)
+
+    @pl.when(span < 8)
+    def _():
+        for group in range(groups):
+            kv[EIGHT, group] = jnp.zeros(kv.shape[2:], jnp.bfloat16)
+
+    for group in range(groups):
+        for which in range(2):
+            kv_local(group, which).wait()
+    start_four(0, 0)
+    wait_kv(0)
+    query_swap(0).start()
+    start_kv(1)
+    start_four(0, 1)
+
+    @pl.when(odd_pair == 0)
+    def _():
+        chain(0, TWO).start()
+
+    @pl.when(odd == 0)
+    def _():
+        chain(0, ONE).start()
+
+    wait_four(0)
+    start_eight(0)
+
+    @pl.when(odd_pair == 1)
+    def _():
+        chain(0, TWO).start()
+
+    start_four(1, 0)
+    wait_kv(1)
+    start_four(1, 1)
+    start_kv(2)
+    query_swap(1).start()
+    chain(0, TWO).wait_recv()
+
+    @pl.when(odd == 1)
+    def _():
+        chain(0, ONE).start()
+
+    for group in range(groups):
+        query_local(group).wait()
+    query_swap(0).wait_recv()
+    chain(0, ONE).wait_recv()
+    wait_eight(0)
+    prepare(0)
+    first = top_of([score_block(0, 0, block) for block in range(4)])
+
+    def one_head(head, top):
+        group = head // sharing
+        turn = head % sharing
+
+        @pl.when(jnp.logical_and(turn == 0, group + 2 < groups))
+        def _():
+            start_four(group + 2, 0)
+            wait_kv(group + 2)
+            start_four(group + 2, 1)
+
+        @pl.when(jnp.logical_and(turn == 0, group + 1 < groups))
+        def _():
+            wait_four(group + 1)
+            start_eight(group + 1)
+            chain(group + 1, TWO).start()
+
+        @pl.when(jnp.logical_and(turn == 2, group + 3 < groups))
+        def _():
+            start_kv(group + 3)
+
+        @pl.when(jnp.logical_and(turn == 2, group + 2 < groups))
+        def _():
+            query_swap(group + 2).start()
+
+        @pl.when(jnp.logical_and(turn == 2, group + 1 < groups))
+        def _():
+            chain(group + 1, TWO).wait_recv()
+            chain(group + 1, ONE).start()
+
+        @pl.when(jnp.logical_and(turn == sharing - 1, group + 1 < groups))
+        def _():
+            query_swap(group + 1).wait_recv()
+            chain(group + 1, ONE).wait_recv()
+            wait_eight(group + 1)
+            prepare(group + 1)
+
+        top = stage(head, 1, head, 0, top)
+        top = stage(jnp.minimum(head + 1, heads - 1), 0, head, 1, top)
+        out_local(head).start()
+        out_swap(head).start()
+        return top
+
+    lax.fori_loop(0, heads, one_head, first)
+
+    def settle_group(group, carry):
+        for which in range(2):
+            kv_swap(group, which).wait_send()
+        query_swap(group).wait_send()
+
+        @pl.when(has_after)
+        def _():
+            four(group, 0).wait_send()
+            four(group, 1).wait_send()
+
+        @pl.when(jnp.logical_and(has_before, has_after))
+        def _():
+            chain(group, EIGHT).wait_send()
+
+        chain(group, TWO).wait_send()
+        chain(group, ONE).wait_send()
+        return carry
+
+    def settle_head(head, carry):
+        out_local(head).wait()
+        out_swap(head).wait_send()
+        out_swap(head).wait_recv()
+        return carry
+
+    lax.fori_loop(0, groups, settle_group, 0)
+    lax.fori_loop(0, heads, settle_head, 0)
+
+
+def fused_attention(choice, query_input, encoded_keys, input_values, spans):
+    rows, width = query_input.shape
+    groups = encoded_keys.shape[1] // HEAD_SIZE // 2
+    heads = width // HEAD_SIZE // 2
+    length = 2 * rows
+    kept = pl.BlockSpec(memory_space=pl.ANY)
+    flops = 4 * 4 * length * length * width // 2
+    dma = pltpu.SemaphoreType.DMA
+    return pl.pallas_call(
+        partial(fused_kernel, spans),
+        out_shape=jax.ShapeDtypeStruct((rows, width), jnp.bfloat16),
+        in_specs=[pl.BlockSpec(memory_space=pltpu.SMEM), kept, kept, kept],
+        out_specs=kept,
+        scratch_shapes=[
+            pltpu.VMEM((5, groups, 2, length, HEAD_SIZE), jnp.bfloat16),
+            pltpu.VMEM((2, rows, heads * HEAD_SIZE), jnp.bfloat16),
+            pltpu.VMEM((2, rows, heads * HEAD_SIZE), jnp.bfloat16),
+            pltpu.VMEM((2, 2, length, HEAD_SIZE), jnp.bfloat16),
+            pltpu.VMEM((2, 4, length, 2 * HEAD_SIZE), jnp.bfloat16),
+            pltpu.VMEM((2, 4, rows, length), jnp.float32),
+            dma((groups,)), dma((groups, 2)),
+            dma((groups,)), dma((groups,)),
+            dma((groups, 2)), dma((groups, 2)),
+            dma((groups, 2)), dma((groups, 2)),
+            dma((groups, 3)), dma((groups, 3)),
+            dma((heads,)), dma((heads,)), dma((heads,)),
+        ],
+        cost_estimate=pl.CostEstimate(
+            flops=flops, bytes_accessed=4 * rows * width, transcendentals=flops // 512
+        ),
+        compiler_params=pltpu.CompilerParams(
+            collective_id=0, has_side_effects=True, vmem_limit_bytes=58 * 1024 * 1024
+        ),
+    )(choice, query_input, encoded_keys, input_values)
+
+
 def per_device(query_input, encoded_keys, input_values, sources):
     head_devices = lax.axis_size("head")
     span_count = lax.axis_size("seq")
@@ -196,6 +575,8 @@
         [(row[column] >= 0).astype(jnp.int32) for column in range(3)]
         + [jnp.clip(slot, 0, len(distances) - 1) for slot in slots]
     )
+    if head_devices == 2 and span_count == 16:
+        return fused_attention(choice, query_input, encoded_keys, input_values, span_count)
     size = min(KEY_HEADS_PER_GROUP, key_heads)
     width = size * HEAD_SIZE
     pieces = [[] for _ in range(head_devices)]

time: 205 us -> 131 us (0.64); the launches traced: 203 us -> 131 us
  waiting for transfers between devices: 66.2 us -> 0 us
  Pallas kernels: 76.6 us -> 119 us
  starting transfers between devices: 25.2 us -> 0 us
  other arithmetic: 18.2 us -> 1.36 us
  local copies, waits for them, and re-layouts: 12 us -> 6.33 us
    ppermute x14 -> x0, waiting for transfers between devices: 66.2 us -> none  [the longest x10 49.7 us: swapped(): lax.ppermute(value, axis, [(i, i ^ distance) for i in range(devices)])]
    pallas_call x2 -> x1, Pallas kernels: 76.6 us -> 119 us  [fused_attention(): pl.pallas_call(partial(fused_kernel, spans), out_shape=jax.ShapeDtypeStru...]
    ppermute x14 -> x0, starting transfers between devices: 25.2 us -> none  [the longest x10 12.7 us: swapped(): lax.ppermute(value, axis, [(i, i ^ distance) for i in range(devices)])]
    select_n x10 -> x0, other arithmetic: 15.5 us -> none  [the longest x4 8.86 us: gather_heads(): jnp.where(mine == 0, jnp.concatenate([kept, arrived], axis=0), jnp.concat...]
    dynamic_slice x4 -> x0, local copies, waits for them, and re-layouts: 8.86 us -> none  [the longest x2 5.33 us: columns(): lax.dynamic_slice_in_dim(array, owner * s + offset * w, w, 1)]
    unnamed x16 -> x1, local copies, waits for them, and re-layouts: 1.99 us -> 4.3 us
    concatenate x3 -> x0, other arithmetic: 2.07 us -> none  [the longest x1 2 us: per_device(): jnp.concatenate([piece for owner in pieces for piece in owner], axis=1)]
  transfers between devices with their start and end apart: 14 -> 0, of which waited for: 6 -> 0; matrix products, arithmetic and copies ran while one was open for 11% -> 0% of each run, Pallas kernels for 38% -> 0%
where the time goes in v2:
time: 131 us
  Pallas kernels  119 us (91%)
  local copies, waits for them, and re-layouts  6.33 us (5%)
  between operations  4.53 us (3%)
  other arithmetic  1.36 us (1%)
    pallas_call x1, Pallas kernels, fused_attention(): pl.pallas_call(partial(fused_kernel, spans), out_shape=jax.ShapeDtypeStru...  119 us
    unnamed x1, local copies, waits for them, and re-layouts  4.3 us

profile of v2, /device:TPU:16, one launch (start us, length us, event | category | flops | bytes accessed | tf_op | source)
XLA Modules:
  0.0 131.1 jit_solution(12319970854880586735)
XLA Ops:
  0.0 1.4 %fusion.2 = (s32[1,1]{1,0:T(1,128)}, s32[1,1]{1,0:T(1,128)}, s32[1,1]{1,0:T(1,128)}) fusion(s32[1,3]{1,0:T(1,128)} %param.8), kind=kLoop, calls=%fused_computation.4 | loop fusion | bytes 24 | tf_op jit(solution)/shard_map/slice | solution.py:575
  4.7 1.4 %fusion.1 = (s32[]{:T(128)}, s32[]{:T(128)}) fusion(s32[3]{0:T(128)} %constant.14.clone, s32[]{:T(128)S(6)} %sub.7, s32[]{:T(128)S(6)} %sub.6), kind=kLoop, calls=%fused_computation.3 | loop fusion | flops 16 | bytes 28 | tf_op jit(solution)/shard_map/reduce_sum | solution.py:572
  7.3 0.6 stack.35.choice_ref
  7.9 118.9 %shard_map.55 = bf16[448,4096]{1,0:T(8,128)(2,1)} custom-call(s32[5]{0:T(128)} %stack.35.choice_ref, bf16[448,4096]{1,0:T(8,128)(2,1)} %query_ref.1, bf16[448,1024]{1,0:T(8,128)(2,1)} %key_ref.1, bf16[448,1024]{1,0:T(8,128)(2,1)} %value_ref.1), custom_call_target="tpu_custom_call" | custom-call | flops 26306674688 | bytes 7340032 | tf_op jit(solution)/shard_map/pallas_call | solution.py:534
  126.8 4.3 %copy.7 = bf16[448,4096]{1,0:T(8,128)(2,1)} copy(bf16[448,4096]{1,0:T(8,128)(2,1)} %shard_map.55) | data formatting | bytes 7340032

commit v3 on v2

--- a/solution.py
+++ b/solution.py
@@ -184,7 +184,7 @@
 
 
 def fused_kernel(
-    spans, choice_ref, query_ref, key_ref, value_ref, out_ref,
+    spans, source_ref, query_ref, key_ref, value_ref, out_ref,
     kv, query_all, result, key_far, value_all, scores,
     local_q, local_kv, send_q, recv_q, send_kv, recv_kv,
     send_four, recv_four, send_chain, recv_chain, local_out, send_out, recv_out,
@@ -261,29 +261,30 @@
             send_four.at[group, step], recv_four.at[group, step], (span + 4, mine),
         )
 
-    def chain(group, slot):
+    def chain(group, slot, step):
         source, device = {
             EIGHT: (FOUR, (span + 4, mine)),
             TWO: (FOUR * odd_pair, (across, mine)),
             ONE: (TWO * odd, (beside, mine)),
         }[slot]
-        index = {ONE: 0, TWO: 1, EIGHT: 2}[slot]
+        index = {ONE: 0, TWO: 2, EIGHT: 4}[slot] + step
+        rows_part = part(mine) if step == 0 else part(other)
         return remote(
-            kv.at[source, group], kv.at[slot, group],
+            kv.at[source, group, :, rows_part, :], kv.at[slot, group, :, rows_part, :],
             send_chain.at[group, index], recv_chain.at[group, index], device,
         )
 
     def out_local(head):
         return pltpu.make_async_copy(
             result.at[mine, :, columns(head, 1)],
-            out_ref.at[:, columns(mine * heads + head, 1)],
+            out_ref.at[mine, :, columns(head, 1)],
             local_out.at[head],
         )
 
     def out_swap(head):
         return remote(
             result.at[other, :, columns(head, 1)],
-            out_ref.at[:, columns(mine * heads + head, 1)],
+            out_ref.at[mine, :, columns(head, 1)],
             send_out.at[head], recv_out.at[head], (span, other),
         )
 
@@ -300,23 +301,23 @@
         def _():
             four(group, step).start()
 
-    def wait_four(group):
+    def wait_four(group, step):
         @pl.when(has_before)
         def _():
-            four(group, 0).wait_recv()
-            four(group, 1).wait_recv()
-
-    def start_eight(group):
+            four(group, step).wait_recv()
+
+    def start_eight(group, step):
         @pl.when(jnp.logical_and(has_before, has_after))
         def _():
-            chain(group, EIGHT).start()
+            chain(group, EIGHT, step).start()
 
     def wait_eight(group):
         @pl.when(span >= 8)
         def _():
-            chain(group, EIGHT).wait_recv()
-
-    valid = [None] + [choice_ref[column] > 0 for column in range(3)]
+            for step in range(2):
+                chain(group, EIGHT, step).wait_recv()
+
+    valid = [None] + [source_ref[0, column] >= 0 for column in range(3)]
     scale = [jnp.float32(EXPONENT_SCALE)] + [
         jnp.where(valid[block], EXPONENT_SCALE, 0.0) for block in range(1, 4)
     ]
@@ -326,10 +327,10 @@
         for block in range(2):
             value_all[side, block, :, :HEAD_SIZE] = kv[block, group, 1]
         for column in range(2):
-            pick = choice_ref[3 + column]
+            away = span - source_ref[0, 1 + column]
             for which in range(2):
-                chosen = lax.select(pick == 1, kv[FOUR, group, which], kv[TWO, group, which])
-                chosen = lax.select(pick == 2, kv[EIGHT, group, which], chosen)
+                chosen = lax.select(away == 4, kv[FOUR, group, which], kv[TWO, group, which])
+                chosen = lax.select(away == 8, kv[EIGHT, group, which], chosen)
                 if which == 0:
                     key_far[side, column] = chosen
                 else:
@@ -408,46 +409,43 @@
         for group in range(groups):
             kv[EIGHT, group] = jnp.zeros(kv.shape[2:], jnp.bfloat16)
 
-    for group in range(groups):
+    for which in range(2):
+        kv_local(0, which).wait()
+
+    def start_chain(slot, step, bit, value):
+        @pl.when(bit == value)
+        def _():
+            chain(0, slot, step).start()
+
+    start_four(0, 0)
+    start_chain(TWO, 0, odd_pair, 0)
+    start_chain(ONE, 0, odd, 0)
+    wait_kv(0)
+    start_four(0, 1)
+    start_chain(TWO, 1, odd_pair, 0)
+    start_chain(ONE, 1, odd, 0)
+    query_swap(0).start()
+    for step in range(2):
+        wait_four(0, step)
+        start_eight(0, step)
+        start_chain(TWO, step, odd_pair, 1)
+    start_kv(1)
+    for step in range(2):
+        chain(0, TWO, step).wait_recv()
+        start_chain(ONE, step, odd, 1)
+    for group in range(1, groups):
         for which in range(2):
             kv_local(group, which).wait()
-    start_four(0, 0)
-    wait_kv(0)
-    query_swap(0).start()
-    start_kv(1)
-    start_four(0, 1)
-
-    @pl.when(odd_pair == 0)
-    def _():
-        chain(0, TWO).start()
-
-    @pl.when(odd == 0)
-    def _():
-        chain(0, ONE).start()
-
-    wait_four(0)
-    start_eight(0)
-
-    @pl.when(odd_pair == 1)
-    def _():
-        chain(0, TWO).start()
-
-    start_four(1, 0)
-    wait_kv(1)
-    start_four(1, 1)
-    start_kv(2)
-    query_swap(1).start()
-    chain(0, TWO).wait_recv()
-
-    @pl.when(odd == 1)
-    def _():
-        chain(0, ONE).start()
-
     for group in range(groups):
         query_local(group).wait()
     query_swap(0).wait_recv()
-    chain(0, ONE).wait_recv()
+    query_swap(1).start()
+    start_four(1, 0)
+    for step in range(2):
+        chain(0, ONE, step).wait_recv()
     wait_eight(0)
+    wait_kv(1)
+    start_four(1, 1)
     prepare(0)
     first = top_of([score_block(0, 0, block) for block in range(4)])
 
@@ -457,37 +455,41 @@
 
         @pl.when(jnp.logical_and(turn == 0, group + 2 < groups))
         def _():
+            start_kv(group + 2)
+
+        @pl.when(jnp.logical_and(turn == 1, group + 2 < groups))
+        def _():
+            query_swap(group + 2).start()
+
+        @pl.when(jnp.logical_and(turn == 1, group + 1 < groups))
+        def _():
+            for step in range(2):
+                wait_four(group + 1, step)
+                start_eight(group + 1, step)
+                chain(group + 1, TWO, step).start()
+
+        @pl.when(jnp.logical_and(turn == sharing - 1, group + 2 < groups))
+        def _():
             start_four(group + 2, 0)
             wait_kv(group + 2)
             start_four(group + 2, 1)
 
-        @pl.when(jnp.logical_and(turn == 0, group + 1 < groups))
-        def _():
-            wait_four(group + 1)
-            start_eight(group + 1)
-            chain(group + 1, TWO).start()
-
-        @pl.when(jnp.logical_and(turn == 2, group + 3 < groups))
-        def _():
-            start_kv(group + 3)
-
-        @pl.when(jnp.logical_and(turn == 2, group + 2 < groups))
-        def _():
-            query_swap(group + 2).start()
-
-        @pl.when(jnp.logical_and(turn == 2, group + 1 < groups))
-        def _():
-            chain(group + 1, TWO).wait_recv()
-            chain(group + 1, ONE).start()
-
         @pl.when(jnp.logical_and(turn == sharing - 1, group + 1 < groups))
         def _():
+            for step in range(2):
+                chain(group + 1, TWO, step).wait_recv()
+                chain(group + 1, ONE, step).start()
+
+        top = stage(head, 1, head, 0, top)
+
+        @pl.when(jnp.logical_and(turn == sharing - 1, group + 1 < groups))
+        def _():
             query_swap(group + 1).wait_recv()
-            chain(group + 1, ONE).wait_recv()
+            for step in range(2):
+                chain(group + 1, ONE, step).wait_recv()
             wait_eight(group + 1)
             prepare(group + 1)
 
-        top = stage(head, 1, head, 0, top)
         top = stage(jnp.minimum(head + 1, heads - 1), 0, head, 1, top)
         out_local(head).start()
         out_swap(head).start()
@@ -505,12 +507,13 @@
             four(group, 0).wait_send()
             four(group, 1).wait_send()
 
-        @pl.when(jnp.logical_and(has_before, has_after))
-        def _():
-            chain(group, EIGHT).wait_send()
-
-        chain(group, TWO).wait_send()
-        chain(group, ONE).wait_send()
+        for step in range(2):
+            @pl.when(jnp.logical_and(has_before, has_after))
+            def _():
+                chain(group, EIGHT, step).wait_send()
+
+            chain(group, TWO, step).wait_send()
+            chain(group, ONE, step).wait_send()
         return carry
 
     def settle_head(head, carry):
@@ -523,7 +526,7 @@
     lax.fori_loop(0, heads, settle_head, 0)
 
 
-def fused_attention(choice, query_input, encoded_keys, input_values, spans):
+def fused_attention(sources, query_input, encoded_keys, input_values, spans):
     rows, width = query_input.shape
     groups = encoded_keys.shape[1] // HEAD_SIZE // 2
     heads = width // HEAD_SIZE // 2
@@ -531,9 +534,9 @@
     kept = pl.BlockSpec(memory_space=pl.ANY)
     flops = 4 * 4 * length * length * width // 2
     dma = pltpu.SemaphoreType.DMA
-    return pl.pallas_call(
+    halves = pl.pallas_call(
         partial(fused_kernel, spans),
-        out_shape=jax.ShapeDtypeStruct((rows, width), jnp.bfloat16),
+        out_shape=jax.ShapeDtypeStruct((2, rows, width // 2), jnp.bfloat16),
         in_specs=[pl.BlockSpec(memory_space=pltpu.SMEM), kept, kept, kept],
         out_specs=kept,
         scratch_shapes=[
@@ -547,7 +550,7 @@
             dma((groups,)), dma((groups,)),
             dma((groups, 2)), dma((groups, 2)),
             dma((groups, 2)), dma((groups, 2)),
-            dma((groups, 3)), dma((groups, 3)),
+            dma((groups, 6)), dma((groups, 6)),
             dma((heads,)), dma((heads,)), dma((heads,)),
         ],
         cost_estimate=pl.CostEstimate(
@@ -556,12 +559,15 @@
         compiler_params=pltpu.CompilerParams(
             collective_id=0, has_side_effects=True, vmem_limit_bytes=58 * 1024 * 1024
         ),
-    )(choice, query_input, encoded_keys, input_values)
+    )(sources, query_input, encoded_keys, input_values)
+    return jnp.transpose(halves, (1, 0, 2)).reshape(rows, width)
 
 
 def per_device(query_input, encoded_keys, input_values, sources):
     head_devices = lax.axis_size("head")
     span_count = lax.axis_size("seq")
+    if head_devices == 2 and span_count == 16:
+        return fused_attention(sources, query_input, encoded_keys, input_values, span_count)
     own_index = lax.axis_index("seq")
     key_heads = encoded_keys.shape[1] // HEAD_SIZE // head_devices
     sharing = query_input.shape[1] // encoded_keys.shape[1]
@@ -575,8 +581,6 @@
         [(row[column] >= 0).astype(jnp.int32) for column in range(3)]
         + [jnp.clip(slot, 0, len(distances) - 1) for slot in slots]
     )
-    if head_devices == 2 and span_count == 16:
-        return fused_attention(choice, query_input, encoded_keys, input_values, span_count)
     size = min(KEY_HEADS_PER_GROUP, key_heads)
     width = size * HEAD_SIZE
     pieces = [[] for _ in range(head_devices)]

time: 131 us -> 130 us (level)
  Pallas kernels: 119 us -> 125 us
  between operations: 4.53 us -> 0.01 us
  local copies, waits for them, and re-layouts: 6.33 us -> 4.37 us
  other arithmetic: 1.36 us -> 0 us
    pallas_call x1, Pallas kernels: 119 us -> 125 us  [fused_attention(): pl.pallas_call(partial(fused_kernel, spans), out_shape=jax.ShapeDtypeStru...]
    reshape x0 -> x1, local copies, waits for them, and re-layouts: none -> 4.37 us  [fused_attention(): return jnp.transpose(halves, (1, 0, 2)).reshape(rows, width)]
    unnamed x1 -> x0, local copies, waits for them, and re-layouts: 4.3 us -> none
    slice x1 -> x0, local copies, waits for them, and re-layouts: 1.43 us -> none  [per_device(): row[column] >= 0]
    reduce_sum x1 -> x0, other arithmetic: 1.36 us -> none  [per_device(): jnp.sum((distance_table < own_index - row[column]).astype(jnp.int32))]
where the time goes in v3:
time: 130 us; the launch traced here: 129 us
  Pallas kernels  125 us (96%)
  local copies, waits for them, and re-layouts  4.37 us (3%)
    pallas_call x1, Pallas kernels, fused_attention(): pl.pallas_call(partial(fused_kernel, spans), out_shape=jax.ShapeDtypeStru...  125 us
    reshape x1, local copies, waits for them, and re-layouts, fused_attention(): return jnp.transpose(halves, (1, 0, 2)).reshape(rows, width)  4.37 us

profile of v3, /device:TPU:16, one launch (start us, length us, event | category | flops | bytes accessed | tf_op | source)
XLA Modules:
  0.0 129.4 jit_solution(14782344984964578452)
XLA Ops:
  0.0 125.0 %shard_map.46 = bf16[2,448,2048]{2,1,0:T(8,128)(2,1)} custom-call(s32[1,3]{1,0:T(1,128)} %source_ref.1, bf16[448,4096]{1,0:T(8,128)(2,1)} %query_ref.1, bf16[448,1024]{1,0:T(8,128)(2,1)} %key_ref.1, bf16[448,1024]{1,0:T(8,128)(2,1)} %value_ref.1), custom_call_target="tpu_custom_call" | custom-call | flops 26306674688 | bytes 7340032 | tf_op jit(solution)/shard_map/pallas_call | solution.py:537
  125.0 4.4 %copy.6 = bf16[2,56,8,2048]{3,2,0,1:T(8,128)(2,1)} copy(bf16[2,56,8,2048]{3,2,1,0:T(8,128)(2,1)} %bitcast.3) | data formatting | bytes 7340032 | tf_op jit(solution)/shard_map/reshape | solution.py:563

commit v4 on v3

--- a/solution.py
+++ b/solution.py
@@ -374,6 +374,11 @@
     def top_of(partials):
         return jnp.max(reduce(jnp.maximum, partials), axis=1, keepdims=True)
 
+    def store(head, tile, total):
+        result[tile, :, columns(head, 1)] = (
+            total[:, :HEAD_SIZE] / total[:, HEAD_SIZE:]
+        ).astype(jnp.bfloat16)
+
     def stage(score_head, score_tile, weigh_head, weigh_tile, top):
         partials = []
         total = None
@@ -381,9 +386,7 @@
             partials.append(score_block(score_head, score_tile, block))
             term = weigh_block(weigh_head, weigh_tile, block, top)
             total = term if total is None else total + term
-        result[weigh_tile, :, columns(weigh_head, 1)] = (
-            total[:, :HEAD_SIZE] / total[:, HEAD_SIZE:]
-        ).astype(jnp.bfloat16)
+        store(weigh_head, weigh_tile, total)
         return top_of(partials)
 
     for group in range(groups):
@@ -447,11 +450,21 @@
     wait_kv(1)
     start_four(1, 1)
     prepare(0)
+    start_kv(2)
     first = top_of([score_block(0, 0, block) for block in range(4)])
+    first = stage(0, 1, 0, 0, first)
 
     def one_head(head, top):
         group = head // sharing
         turn = head % sharing
+
+        @pl.when(turn == 0)
+        def _():
+            query_swap(group).wait_recv()
+            for step in range(2):
+                chain(group, ONE, step).wait_recv()
+            wait_eight(group)
+            prepare(group)
 
         @pl.when(jnp.logical_and(turn == 0, group + 2 < groups))
         def _():
@@ -468,7 +481,7 @@
                 start_eight(group + 1, step)
                 chain(group + 1, TWO, step).start()
 
-        @pl.when(jnp.logical_and(turn == sharing - 1, group + 2 < groups))
+        @pl.when(jnp.logical_and(turn == sharing - 2, group + 2 < groups))
         def _():
             start_four(group + 2, 0)
             wait_kv(group + 2)
@@ -480,22 +493,18 @@
                 chain(group + 1, TWO, step).wait_recv()
                 chain(group + 1, ONE, step).start()
 
+        top = stage(head, 0, head - 1, 1, top)
         top = stage(head, 1, head, 0, top)
-
-        @pl.when(jnp.logical_and(turn == sharing - 1, group + 1 < groups))
-        def _():
-            query_swap(group + 1).wait_recv()
-            for step in range(2):
-                chain(group + 1, ONE, step).wait_recv()
-            wait_eight(group + 1)
-            prepare(group + 1)
-
-        top = stage(jnp.minimum(head + 1, heads - 1), 0, head, 1, top)
-        out_local(head).start()
-        out_swap(head).start()
+        out_local(head - 1).start()
+        out_swap(head - 1).start()
         return top
 
-    lax.fori_loop(0, heads, one_head, first)
+    last = lax.fori_loop(1, heads, one_head, first)
+    store(
+        heads - 1, 1, reduce(jnp.add, [weigh_block(heads - 1, 1, block, last) for block in range(4)])
+    )
+    out_local(heads - 1).start()
+    out_swap(heads - 1).start()
 
     def settle_group(group, carry):
         for which in range(2):

time: 130 us -> 119 us (0.915)
  Pallas kernels: 125 us -> 113 us
    pallas_call x1, Pallas kernels: 125 us -> 113 us  [fused_attention(): pl.pallas_call(partial(fused_kernel, spans), out_shape=jax.ShapeDtypeStru...]
where the time goes in v4:
time: 119 us; the launch traced here: 118 us
  Pallas kernels  113 us (95%)
  local copies, waits for them, and re-layouts  4.37 us (4%)
    pallas_call x1, Pallas kernels, fused_attention(): pl.pallas_call(partial(fused_kernel, spans), out_shape=jax.ShapeDtypeStru...  113 us
    reshape x1, local copies, waits for them, and re-layouts, fused_attention(): return jnp.transpose(halves, (1, 0, 2)).reshape(rows, width)  4.37 us

profile of v4, /device:TPU:16, one launch (start us, length us, event | category | flops | bytes accessed | tf_op | source)
XLA Modules:
  0.0 117.7 jit_solution(3233726841856767612)
XLA Ops:
  0.0 113.3 %shard_map.46 = bf16[2,448,2048]{2,1,0:T(8,128)(2,1)} custom-call(s32[1,3]{1,0:T(1,128)} %source_ref.1, bf16[448,4096]{1,0:T(8,128)(2,1)} %query_ref.1, bf16[448,1024]{1,0:T(8,128)(2,1)} %key_ref.1, bf16[448,1024]{1,0:T(8,128)(2,1)} %value_ref.1), custom_call_target="tpu_custom_call" | custom-call | flops 26306674688 | bytes 7340032 | tf_op jit(solution)/shard_map/pallas_call | solution.py:546
  113.3 4.4 %copy.6 = bf16[2,56,8,2048]{3,2,0,1:T(8,128)(2,1)} copy(bf16[2,56,8,2048]{3,2,1,0:T(8,128)(2,1)} %bitcast.3) | data formatting | bytes 7340032 | tf_op jit(solution)/shard_map/reshape | solution.py:572

commit v5 on v4

--- a/solution.py
+++ b/solution.py
@@ -348,9 +348,12 @@
             query, key, (((1,), (1,)), ((), ())), preferred_element_type=jnp.float32
         )
         if block == 0:
-            row = lax.broadcasted_iota(jnp.int32, scored.shape, 0) + tile * rows
-            column = lax.broadcasted_iota(jnp.int32, scored.shape, 1)
-            scored = jnp.where(column <= row, scored, negative_fill)
+            start = tile * rows // LANES * LANES
+            edge = scored[:, start:]
+            row = lax.broadcasted_iota(jnp.int32, edge.shape, 0) + tile * rows
+            column = lax.broadcasted_iota(jnp.int32, edge.shape, 1) + start
+            edge = jnp.where(column <= row, edge, negative_fill)
+            scored = jnp.concatenate([scored[:, :start], edge], axis=1) if start else edge
         scores[tile, block, :, :width] = scored
         partial_top = reduce(
             jnp.maximum, [scored[:, i : i + LANES] for i in range(0, width, LANES)]
@@ -442,7 +445,7 @@
     for group in range(groups):
         query_local(group).wait()
     query_swap(0).wait_recv()
-    query_swap(1).start()
+    start_kv(2)
     start_four(1, 0)
     for step in range(2):
         chain(0, ONE, step).wait_recv()
@@ -450,7 +453,7 @@
     wait_kv(1)
     start_four(1, 1)
     prepare(0)
-    start_kv(2)
+    query_swap(1).start()
     first = top_of([score_block(0, 0, block) for block in range(4)])
     first = stage(0, 1, 0, 0, first)
 
@@ -466,11 +469,11 @@
             wait_eight(group)
             prepare(group)
 
-        @pl.when(jnp.logical_and(turn == 0, group + 2 < groups))
-        def _():
-            start_kv(group + 2)
-
-        @pl.when(jnp.logical_and(turn == 1, group + 2 < groups))
+        @pl.when(jnp.logical_and(turn == 1, group + 3 < groups))
+        def _():
+            start_kv(group + 3)
+
+        @pl.when(jnp.logical_and(turn == sharing - 1, group + 2 < groups))
         def _():
             query_swap(group + 2).start()
 

time: 119 us -> 115 us (0.966)
  Pallas kernels: 113 us -> 110 us
    pallas_call x1, Pallas kernels: 113 us -> 110 us  [fused_attention(): pl.pallas_call(partial(fused_kernel, spans), out_shape=jax.ShapeDtypeStru...]
where the time goes in v5:
time: 115 us; the launch traced here: 114 us
  Pallas kernels  110 us (96%)
  local copies, waits for them, and re-layouts  4.37 us (4%)
    pallas_call x1, Pallas kernels, fused_attention(): pl.pallas_call(partial(fused_kernel, spans), out_shape=jax.ShapeDtypeStru...  110 us
    reshape x1, local copies, waits for them, and re-layouts, fused_attention(): return jnp.transpose(halves, (1, 0, 2)).reshape(rows, width)  4.37 us

profile of v5, /device:TPU:16, one launch (start us, length us, event | category | flops | bytes accessed | tf_op | source)
XLA Modules:
  0.0 114.3 jit_solution(5476911136464449226)
XLA Ops:
  0.0 110.0 %shard_map.46 = bf16[2,448,2048]{2,1,0:T(8,128)(2,1)} custom-call(s32[1,3]{1,0:T(1,128)} %source_ref.1, bf16[448,4096]{1,0:T(8,128)(2,1)} %query_ref.1, bf16[448,1024]{1,0:T(8,128)(2,1)} %key_ref.1, bf16[448,1024]{1,0:T(8,128)(2,1)} %value_ref.1), custom_call_target="tpu_custom_call" | custom-call | flops 26306674688 | bytes 7340032 | tf_op jit(solution)/shard_map/pallas_call | solution.py:549
  110.0 4.4 %copy.6 = bf16[2,56,8,2048]{3,2,0,1:T(8,128)(2,1)} copy(bf16[2,56,8,2048]{3,2,1,0:T(8,128)(2,1)} %bitcast.3) | data formatting | bytes 7340032 | tf_op jit(solution)/shard_map/reshape | solution.py:575
